TPU v7x, 32 devices: a whole 2x2x4 slice. The times are simulated.
32 devices in a mesh: band: 16 (over z, x, core), domain: 2 (over y).
Axes of the slice: x: 2, y: 2, z: 4, core: 2. Of those that a mesh axis runs over, the one named last changes fastest.
Arguments:
- orbitals: float32 [256, 16, 4096], P('band', 'domain'), may hold values from -6 to 6
- previous: float32 [256, 16, 4096], P('band', 'domain'), may hold values from -6 to 6
- potential: float32 [16, 4096], P('domain'), may hold values from -3 to 3
- rotation: float32 [256, 256], P(None, 'band'), may hold values from -1 to 1
- accumulated: float32 [256, 16, 4096], P('band', 'domain'), may hold values from -6 to 6
- panel: int32 [1], replicated, may hold values from 0 to 65535
Outputs:
- filtered: float32 [256, 16, 4096], P('band', 'domain')
- rotated: float32 [256, 16, 4096], P('band', 'domain')
All inputs are finite; a program needn't handle non-finite values.
Results may differ from a plain program's by a relative error of at most 0.000059.
Values sent between devices are 32-bit elements; how exact they have to be, the bound alone decides.
A program may use at most 192 MiB of HBM per device.

v0:
```python
import jax
import jax.numpy as jnp
from jax import lax
from jax.sharding import PartitionSpec as P

NX = 64


coefs = (
    -5369.0 / 1800.0,
    12.0 / 7.0,
    -15.0 / 56.0,
    10.0 / 189.0,
    -1.0 / 112.0,
    2.0 / 1925.0,
    -1.0 / 16632.0,
)


def padded_2(cells, sides, width):
    for axis, dim in sides:
        count = lax.axis_size(axis)
        head = lax.slice_in_dim(cells, 0, width, axis=dim)
        tail = lax.slice_in_dim(cells, cells.shape[dim] - width, cells.shape[dim], axis=dim)
        cells = jnp.concatenate(
            [
                lax.ppermute(tail, axis, [(i, (i + 1) % count) for i in range(count)]),
                cells,
                lax.ppermute(head, axis, [((i + 1) % count, i) for i in range(count)]),
            ],
            axis=dim,
        )
    return cells


def from_root(block, axis, owner):
    block = jnp.where(lax.axis_index(axis) == owner, block, jnp.zeros_like(block))
    return lax.psum(block, axis)


def add_panel(total, rows, block):
    flat = block.reshape(block.shape[0], -1)
    product = lax.dot_general(
        rows,
        flat,
        (((0,), (0,)), ((), ())),
        precision=lax.Precision.HIGHEST,
        preferred_element_type=jnp.float32,
    )
    return total + product.reshape(total.shape)


def shift_x(values, amount, column):
    if amount > 0:
        return jnp.where(
            column >= amount, jnp.roll(values, amount, 2), jnp.roll(values, amount - NX, 2)
        )
    return jnp.where(
        column < NX + amount, jnp.roll(values, amount, 2), jnp.roll(values, amount + NX, 2)
    )


def local(orbitals, previous, potential, rotation, accumulated, panel):
    planes = orbitals.shape[1]
    cells = orbitals.shape[2]
    column = (lax.iota(jnp.int32, cells) % NX)[None, None, :]
    padded = padded_2(orbitals, (("domain", 1),), 6)
    lap = 3.0 * coefs[0] * orbitals
    for step in range(1, 7):
        lap = lap + coefs[step] * (
            padded[:, 6 + step : 6 + step + planes] + padded[:, 6 - step : 6 - step + planes]
        )
        lap = lap + coefs[step] * (
            jnp.roll(orbitals, step * NX, 2) + jnp.roll(orbitals, -step * NX, 2)
        )
        lap = lap + coefs[step] * (
            shift_x(orbitals, step, column) + shift_x(orbitals, -step, column)
        )
    ham = -2.0 * lap + potential[None] * orbitals
    filtered = (ham - 36.0 * orbitals) / 14.0 - previous
    orb_count = orbitals.shape[0]
    pairs = lax.axis_size("band") // 2
    first_root = 2 * (panel[0] % pairs)
    rows = lax.dynamic_slice_in_dim(rotation, first_root * orb_count, 2 * orb_count, 0)
    rotated = accumulated
    for member in range(2):
        block = from_root(filtered, "band", first_root + member)
        rotated = add_panel(rotated, rows[member * orb_count : (member + 1) * orb_count], block)
    return (filtered, rotated)


def solution(mesh):
    in_specs = (
        P("band", "domain", None),
        P("band", "domain", None),
        P("domain", None),
        P(None, "band"),
        P("band", "domain", None),
        P(),
    )
    out_specs = (P("band", "domain", None), P("band", "domain", None))
    return jax.shard_map(local, mesh=mesh, in_specs=in_specs, out_specs=out_specs, check_vma=False)
```

profile of v0, /device:TPU:1, one launch (start us, length us, event | category | flops | bytes accessed | tf_op | source)
XLA Modules:
  0.0 249.2 jit_solution(8560357731123557221)
XLA Ops:
  7.2 0.0 copy-start
  7.2 0.0 all-reduce.3.cloned.1.call-start
  7.2 2.6 %fusion.106 = (f32[16,6,4096]{2,1,0:T(8,128)S(1)}, f32[16,6,4096]{2,1,0:T(8,128)S(1)}) fusion(f32[16,8,4096]{2,1,0:T(8,128)} %param.6), kind=kLoop, calls=%fused_computation.146 | loop fusion | bytes 6291456 | tf_op jit(solution)/shard_map/slice | solution.py:23
  9.9 2.1 copy.22
  12.0 2.1 collective-permute-start
  14.0 2.1 copy.23
  16.1 0.0 collective-permute-start.1
  16.1 0.0 copy-done.1
  16.1 2.7 %fusion.77 = (f32[16,8,4032]{2,1,0:T(8,128)}, f32[16,8,4032]{2,1,0:T(8,128)}) fusion(f32[16,8,4096]{2,1,0:T(8,128)S(1)} %copy-done.1), kind=kLoop, calls=%fused_computation.117 | loop fusion | bytes 8257536 | tf_op jit(solution)/shard_map/jit(_roll_static)/slice | solution.py:74
  18.8 2.7 %fusion.79 = (f32[16,8,4095]{2,1,0:T(8,128)}, f32[16,8,4095]{2,1,0:T(8,128)}) fusion(f32[16,8,4096]{2,1,0:T(8,128)S(1)} %copy-done.1), kind=kLoop, calls=%fused_computation.119 | loop fusion | bytes 8386560 | tf_op jit(solution)/shard_map/jit(_roll_static)/slice | solution.py:56
  21.6 2.7 %fusion.80 = (f32[16,8,4033]{2,1,0:T(8,128)}, f32[16,8,4033]{2,1,0:T(8,128)}) fusion(f32[16,8,4096]{2,1,0:T(8,128)S(1)} %copy-done.1), kind=kLoop, calls=%fused_computation.120 | loop fusion | bytes 8259584 | tf_op jit(solution)/shard_map/jit(_roll_static)/slice | solution.py:56
  24.3 2.8 %fusion.85 = (f32[16,8,4094]{2,1,0:T(8,128)}, f32[16,8,4094]{2,1,0:T(8,128)}) fusion(f32[16,8,4096]{2,1,0:T(8,128)S(1)} %copy-done.1), kind=kLoop, calls=%fused_computation.125 | loop fusion | bytes 8384512 | tf_op jit(solution)/shard_map/jit(_roll_static)/slice | solution.py:56
  27.1 2.7 %fusion.86 = (f32[16,8,4034]{2,1,0:T(8,128)}, f32[16,8,4034]{2,1,0:T(8,128)}) fusion(f32[16,8,4096]{2,1,0:T(8,128)S(1)} %copy-done.1), kind=kLoop, calls=%fused_computation.126 | loop fusion | bytes 8261632 | tf_op jit(solution)/shard_map/jit(_roll_static)/slice | solution.py:56
  29.8 2.7 %fusion.91 = (f32[16,8,4093]{2,1,0:T(8,128)}, f32[16,8,4093]{2,1,0:T(8,128)}) fusion(f32[16,8,4096]{2,1,0:T(8,128)S(1)} %copy-done.1), kind=kLoop, calls=%fused_computation.131 | loop fusion | bytes 8382464 | tf_op jit(solution)/shard_map/jit(_roll_static)/slice | solution.py:56
  32.5 2.7 %fusion.92 = (f32[16,8,4035]{2,1,0:T(8,128)}, f32[16,8,4035]{2,1,0:T(8,128)}) fusion(f32[16,8,4096]{2,1,0:T(8,128)S(1)} %copy-done.1), kind=kLoop, calls=%fused_computation.132 | loop fusion | bytes 8263680 | tf_op jit(solution)/shard_map/jit(_roll_static)/slice | solution.py:56
  35.2 2.8 %fusion.97 = (f32[16,8,4092]{2,1,0:T(8,128)}, f32[16,8,4092]{2,1,0:T(8,128)}) fusion(f32[16,8,4096]{2,1,0:T(8,128)S(1)} %copy-done.1), kind=kLoop, calls=%fused_computation.137 | loop fusion | bytes 8380416 | tf_op jit(solution)/shard_map/jit(_roll_static)/slice | solution.py:56
  38.0 2.7 %fusion.98 = (f32[16,8,4036]{2,1,0:T(8,128)}, f32[16,8,4036]{2,1,0:T(8,128)}) fusion(f32[16,8,4096]{2,1,0:T(8,128)S(1)} %copy-done.1), kind=kLoop, calls=%fused_computation.138 | loop fusion | bytes 8265728 | tf_op jit(solution)/shard_map/jit(_roll_static)/slice | solution.py:56
  40.6 2.7 %fusion.103 = (f32[16,8,4091]{2,1,0:T(8,128)}, f32[16,8,4091]{2,1,0:T(8,128)}) fusion(f32[16,8,4096]{2,1,0:T(8,128)S(1)} %copy-done.1), kind=kLoop, calls=%fused_computation.143 | loop fusion | bytes 8378368 | tf_op jit(solution)/shard_map/jit(_roll_static)/slice | solution.py:56
  43.3 2.7 %fusion.104 = (f32[16,8,4037]{2,1,0:T(8,128)}, f32[16,8,4037]{2,1,0:T(8,128)}) fusion(f32[16,8,4096]{2,1,0:T(8,128)S(1)} %copy-done.1), kind=kLoop, calls=%fused_computation.144 | loop fusion | bytes 8267776 | tf_op jit(solution)/shard_map/jit(_roll_static)/slice | solution.py:56
  46.0 2.8 %fusion.110 = (f32[16,8,4090]{2,1,0:T(8,128)}, f32[16,8,4090]{2,1,0:T(8,128)}) fusion(f32[16,8,4096]{2,1,0:T(8,128)S(1)} %copy-done.1), kind=kLoop, calls=%fused_computation.150 | loop fusion | bytes 8376320 | tf_op jit(solution)/shard_map/jit(_roll_static)/slice | solution.py:56
  48.8 2.7 %fusion.111 = (f32[16,8,4038]{2,1,0:T(8,128)}, f32[16,8,4038]{2,1,0:T(8,128)}) fusion(f32[16,8,4096]{2,1,0:T(8,128)S(1)} %copy-done.1), kind=kLoop, calls=%fused_computation.151 | loop fusion | bytes 8269824 | tf_op jit(solution)/shard_map/jit(_roll_static)/slice | solution.py:56
  51.5 2.2 fusion.83
  53.7 2.7 %fusion.89 = (f32[16,8,3904]{2,1,0:T(8,128)}, f32[16,8,3904]{2,1,0:T(8,128)}) fusion(f32[16,8,4096]{2,1,0:T(8,128)S(1)} %copy-done.1), kind=kLoop, calls=%fused_computation.129 | loop fusion | bytes 7995392 | tf_op jit(solution)/shard_map/jit(_roll_static)/slice | solution.py:74
  56.4 2.3 fusion.95
  58.7 2.5 %fusion.101 = (f32[16,8,3776]{2,1,0:T(8,128)}, f32[16,8,3776]{2,1,0:T(8,128)}) fusion(f32[16,8,4096]{2,1,0:T(8,128)S(1)} %copy-done.1), kind=kLoop, calls=%fused_computation.141 | loop fusion | bytes 7733248 | tf_op jit(solution)/shard_map/jit(_roll_static)/slice | solution.py:74
  61.3 0.1 fusion.100
  61.4 0.7 fusion.88
  62.1 0.7 fusion.94
  62.8 0.6 fusion.76
  63.4 0.7 fusion.78
  64.1 0.7 fusion.81
  64.8 0.7 fusion.82
  65.5 0.7 fusion.84
  66.2 0.7 fusion.87
  66.9 0.7 fusion.90
  67.6 0.7 fusion.93
  68.4 0.7 fusion.96
  69.1 0.7 fusion.99
  69.8 0.7 fusion.102
  70.5 0.7 fusion.105
  71.2 0.7 fusion.109
  71.9 0.7 fusion.112
  73.4 0.1 constant_dynamic-update-slice_fusion
  73.6 2.1 fusion.108
  75.6 6.5 %collective-permute-done.1 = f32[16,6,4096]{2,0,1:T(8,128)} collective-permute-done((f32[16,6,4096]{2,0,1:T(8,128)}, f32[16,6,4096]{2,0,1:T(8,128)}, u32[]{:S(2)}, u32[]{:S(2)}) %collective-permute-start.1) | collective-permute-done | bytes 1572896 | tf_op jit(solution)/shard_map/ppermute | solution.py:27
  82.2 2.5 %copy.17 = f32[16,6,4096]{2,1,0:T(8,128)S(1)} copy(f32[16,6,4096]{2,0,1:T(8,128)} %collective-permute-done.1) | data formatting | bytes 3145728 | tf_op jit(solution)/shard_map/ppermute | solution.py:27
  84.7 0.0 copy-start.3
  84.7 0.0 collective-permute-done
  84.7 2.5 %copy_dynamic-update-slice_fusion = f32[16,14,4096]{2,1,0:T(8,128)S(1)} fusion(f32[16,14,4096]{2,1,0:T(8,128)S(1)} %constant_dynamic-update-slice_fusion, f32[16,6,4096]{2,0,1:T(8,128)} %collective-permute-done), kind=kLoop, calls=%fused_computation.91 | loop fusion | bytes 3670016 | tf_op jit(solution)/shard_map/concatenate | solution.py:25
  87.2 0.0 copy-done.4
  87.2 0.0 copy-done.3
  87.2 26.4 %broadcast_select_fusion = (f32[16,8,4096]{2,1,0:T(8,128)S(1)}, f32[16,8,4096]{2,1,0:T(8,128)S(1)}) fusion(pred[]{:T(512)S(6)} %eq.11, f32[16,8,4096]{2,1,0:T(8,128)} %param.7, f32[16,8,4096]{2,1,0:T(8,128)S(1)} %copy-done.1, f32[8,4096]{1,0:T(8,128)} %param.8, f32[16,8,4038]{2,1,0:T(8,128)} %get-tuple-element.83, f32[16,8,58]{2,1,0:T(8,128)} %get-tuple-element.85, ...), kind=kLoop, calls=%fused_computation.92 | loop fusion | flops 61341696 | bytes 98222080 | tf_op jit(solution)/shard_map/jit(_where)/select_n | solution.py:37
  113.6 0.0 copy-start.2
  113.6 0.2 broadcast_select_fusion.1
  113.8 1.1 copy-done.2
  115.0 2.5 %copy_bitcast_fusion.1 = f32[8,4096,16]{1,2,0:T(8,128)} fusion(f32[2,8,8,4096]{3,2,1,0:T(8,128)S(1)} %bitcast.31), kind=kLoop, calls=%fused_computation.51 | loop fusion | bytes 4194304 | tf_op jit(solution)/shard_map/dot_general | solution.py:43
  117.5 2.6 %copy_bitcast_fusion = f32[8,4096,16]{1,2,0:T(8,128)} fusion(f32[2,8,8,4096]{3,2,1,0:T(8,128)S(1)} %bitcast.30), kind=kLoop, calls=%fused_computation.50 | loop fusion | bytes 4194304 | tf_op jit(solution)/shard_map/dot_general | solution.py:43
  120.1 0.0 all-reduce.3.cloned.1.call-update
  120.1 112.4 %all-reduce.3.cloned.1.call-done = (f32[8,4096,16]{1,2,0:T(8,128)}, f32[8,4096,16]{1,2,0:T(8,128)}) async-done(((f32[8,4096,16]{1,2,0:T(8,128)}, f32[8,4096,16]{1,2,0:T(8,128)}), (f32[8,4096,16]{1,2,0:T(8,128)}, f32[8,4096,16]{1,2,0:T(8,128)})) %all-reduce.3.cloned.1.call-update) | async-done | bytes 4194320 | tf_op jit(solution)/shard_map/psum | solution.py:38
  232.5 0.0 copy-done
  232.5 5.3 %convolution_add_fusion.1 = f32[16,8,4096]{2,0,1:T(8,128)S(1)} fusion(f32[8,4096,16]{1,2,0:T(8,128)} %get-tuple-element.8, f32[16,8,4096]{2,1,0:T(8,128)} %param.10, f32[256,16]{0,1:T(8,128)S(1)} %copy-done, s32[]{:T(128)S(6)} %select_n.140), kind=kOutput, calls=%fused_computation.11 | convolution fusion | flops 101187584 | bytes 6299652 | tf_op jit(solution)/shard_map/dot_general | solution.py:43
  237.8 0.0 copy-done.5
  237.8 2.0 convolution_add_fusion
  239.8 2.5 %copy.21 = f32[16,8,4096]{2,1,0:T(8,128)} copy(f32[16,8,4096]{2,0,1:T(8,128)S(1)} %convolution_add_fusion) | data formatting | bytes 4194304
  (10 shorter events, 0.1 us)
Async XLA Ops:
  7.2 225.3 %copy-start = (f32[256,16]{0,1:T(8,128)S(1)}, f32[256,16]{0,1:T(8,128)}, u32[]{:S(2)}) copy-start(f32[256,16]{0,1:T(8,128)} %param.9) | copy-start | bytes 49156
  7.2 225.3 %all-reduce.3.cloned.1.call-start = ((), (), s32[]{:S(2)}) async-start(), calls=%async_computation | async-start | bytes 8388608 | tf_op jit(solution)/shard_map/psum | solution.py:38
  12.0 4.2 %copy-start.1 = (f32[16,8,4096]{2,1,0:T(8,128)S(1)}, f32[16,8,4096]{2,1,0:T(8,128)}, u32[]{:S(2)}) copy-start(f32[16,8,4096]{2,1,0:T(8,128)} %param.6) | copy-start | bytes 6291460
  12.0 72.7 %collective-permute-start = (f32[16,6,4096]{2,0,1:T(8,128)}, f32[16,6,4096]{2,0,1:T(8,128)}, u32[]{:S(2)}, u32[]{:S(2)}) collective-permute-start(f32[16,6,4096]{2,0,1:T(8,128)} %copy.22), channel_id=1, source_target_pairs={{1,0},{0,1},{3,2},{2,3},{5,4},{4,5},{7,6},{6,7},{9,8},{8,9},{11,10... | collective-permute-start | bytes 4718600 | tf_op jit(solution)/shard_map/ppermute | solution.py:29
  16.1 66.0 %collective-permute-start.1 = (f32[16,6,4096]{2,0,1:T(8,128)}, f32[16,6,4096]{2,0,1:T(8,128)}, u32[]{:S(2)}, u32[]{:S(2)}) collective-permute-start(f32[16,6,4096]{2,0,1:T(8,128)} %copy.23), channel_id=1, source_target_pairs={{0,1},{1,0},{2,3},{3,2},{4,5},{5,4},{6,7},{7,6},{8,9},{9,8},{10,11... | collective-permute-start | bytes 4718600 | tf_op jit(solution)/shard_map/ppermute | solution.py:27
  82.2 5.0 %copy-start.4 = (f32[16,8,4032]{2,1,0:T(8,128)S(1)}, f32[16,8,4032]{2,1,0:T(8,128)}, u32[]{:S(2)}) copy-start(f32[16,8,4032]{2,1,0:T(8,128)} %get-tuple-element.15) | copy-start | bytes 6193156
  84.7 2.5 %copy-start.3 = (f32[16,8,4032]{2,1,0:T(8,128)S(1)}, f32[16,8,4032]{2,1,0:T(8,128)}, u32[]{:S(2)}) copy-start(f32[16,8,4032]{2,1,0:T(8,128)} %get-tuple-element.14) | copy-start | bytes 6193156
  113.6 1.3 copy-start.2
  232.5 5.3 %copy-start.5 = (f32[8,4096,16]{1,2,0:T(8,128)S(1)}, f32[8,4096,16]{1,2,0:T(8,128)}, u32[]{:S(2)}) copy-start(f32[8,4096,16]{1,2,0:T(8,128)} %get-tuple-element.9) | copy-start | bytes 6291460
Sparse Core Ops, SparseCore 0:
  120.2 112.2 all-reduce.2
where the time goes:
time: 251 us; the launch traced here: 249 us
  waiting for transfers between devices  119 us (47%)
  local copies, waits for them, and re-layouts  79.3 us (32%)
  other arithmetic  26.6 us (11%)
  between operations  14.9 us (6%)
  matrix products  7.3 us (3%)
    psum x1, waiting for transfers between devices, from_root(): return lax.psum(block, axis)  112 us
    select_n x2, other arithmetic, from_root(): jnp.where(lax.axis_index(axis) == owner, block, jnp.zeros_like(block))  26.6 us
    slice x12, local copies, waits for them, and re-layouts, shift_x(): jnp.roll(values, amount, 2)  20.7 us
    slice x12, local copies, waits for them, and re-layouts, shift_x(): jnp.roll(values, amount - NX, 2)  20.5 us
    slice x12, local copies, waits for them, and re-layouts, local(): jnp.roll(orbitals, step * NX, 2) + jnp.roll(orbitals, -step * NX, 2)  17.4 us
    unnamed x16, local copies, waits for them, and re-layouts  8.03 us
    dot_general x2, matrix products, add_panel(): lax.dot_general(rows, flat, (((0,), (0,)), ((), ())), precision=lax.Preci...  7.3 us
    ppermute x1, waiting for transfers between devices, padded_2(): lax.ppermute(tail, axis, [(i, (i + 1) % count) for i in range(count)])  6.53 us
  transfers between devices with their start and end apart: 3, of which 2 were waited for; matrix products, arithmetic and copies ran while one was open for 25% of the time, Pallas kernels for 0%

commit v1 on v0

v1 whole, which is shorter than its diff:
```python
import functools

import jax
import jax.numpy as jnp
import numpy as np
from jax import lax
from jax.experimental import pallas as pl
from jax.experimental.pallas import tpu as pltpu
from jax.sharding import PartitionSpec as P

NX = 64
REACH = 6
LANES = 128
PAD = REACH * NX
PARTS = 2
WINDOW = 6
LAG_X = 2
LAG_Z = 2
LAG_C = 2
MESH = pl.DeviceIdType.MESH

coefs = (
    -5369.0 / 1800.0,
    12.0 / 7.0,
    -15.0 / 56.0,
    10.0 / 189.0,
    -1.0 / 112.0,
    2.0 / 1925.0,
    -1.0 / 16632.0,
)
scaled = tuple(-c / 7.0 for c in coefs)


def z_tables(planes, domains):
    def weight(distance):
        distance = abs(distance)
        return scaled[distance] if 0 < distance <= REACH else 0.0

    own = np.zeros((planes, planes))
    lower = np.zeros((planes, planes))
    upper = np.zeros((planes, planes))
    for r in range(planes):
        for z in range(planes):
            j = (z - r) % planes
            own[r, z] = 3.0 * scaled[0] if j == z else weight(j - z)
            lower[r, z] = weight(j - planes - z)
            upper[r, z] = weight(j + planes - z)
    sets = [own, lower + upper] if domains == 2 else [own, lower, upper]
    table = np.stack(sets).astype(np.float32)
    return np.broadcast_to(table[..., None], table.shape + (LANES,)).copy()


def x_matrix():
    matrix = np.zeros((LANES, LANES), np.float64)
    for col in range(LANES):
        base = col // NX * NX
        for step in range(1, REACH + 1):
            for sign in (1, -1):
                matrix[base + (col - base + sign * step) % NX, col] += scaled[step]
    return matrix.astype(np.float32)


def kernel(
    domains, bands,
    sel, rows, orb, prev, pot, acc, table, xmat,
    out, rot,
    own, prv, total, fil, halo, from_x, right, left, block, other,
    in_sem, h_send, h_recv, x_send, x_recv, r_send, r_recv, l_send, l_recv,
    c_send, c_recv, o_sem, t_sem,
):
    orbs, planes, cells = orb.shape
    width = cells // PARTS
    count = orbs * PARTS
    lines = bands // 4
    sides = 1 if domains == 2 else 2

    d = lax.axis_index("domain")
    b = lax.axis_index("band")
    core = b % 2
    px = (b // 2) % 2
    pz = b // 4
    core_to = b + 1 - 2 * core
    x_to = b + 2 - 4 * px
    z_up = b + 4
    z_down = b - 4
    d_up = (d + 1) % domains
    d_down = (d + domains - 1) % domains
    d_to = (d_up,) if sides == 1 else (d_up, d_down)

    has_up = pz < lines - 1
    has_down = pz > 0

    def at(ref, i):
        return ref.at[i % orbs, :, pl.ds(pl.multiple_of(i // orbs * width, LANES), width)]

    def load(ref, i):
        return ref[i % orbs, :, pl.ds(pl.multiple_of(i // orbs * width, LANES), width)]

    def store(ref, i, value):
        ref[i % orbs, :, pl.ds(pl.multiple_of(i // orbs * width, LANES), width)] = value

    def remote(src, dst, ss, rs, to):
        return pltpu.make_async_remote_copy(
            src_ref=src, dst_ref=dst, send_sem=ss, recv_sem=rs,
            device_id={"domain": to[0], "band": to[1]}, device_id_type=MESH,
        )

    def halo_copy(s, i):
        return remote(at(orb, i), at(halo.at[s], i), h_send.at[s, i], h_recv.at[s, i], (d_to[s], b))

    def x_copy(i):
        return remote(at(fil, i), at(from_x, i), x_send.at[i], x_recv.at[i], (d, x_to))

    def right_copy(i):
        return remote(at(right, i), at(right, i), r_send.at[i], r_recv.at[i], (d, z_up))

    def left_copy(i):
        return remote(at(left, i), at(left, i), l_send.at[i], l_recv.at[i], (d, z_down))

    def core_copy(i):
        return remote(at(block, i), at(other, i), c_send.at[i], c_recv.at[i], (d, core_to))

    def out_copy(i):
        return pltpu.make_async_copy(at(fil, i), at(out, i), o_sem.at[i])

    def total_copy(p):
        part = pl.ds(p * width, width)
        return pltpu.make_async_copy(total.at[:, :, part], rot.at[:, :, part], t_sem.at[p])

    loads = [
        pltpu.make_async_copy(orb, own.at[:, :, pl.ds(PAD, cells)], in_sem.at[0]),
        pltpu.make_async_copy(
            orb.at[:, :, pl.ds(cells - PAD, PAD)], own.at[:, :, pl.ds(0, PAD)], in_sem.at[1]
        ),
        pltpu.make_async_copy(
            orb.at[:, :, pl.ds(0, PAD)], own.at[:, :, pl.ds(PAD + cells, PAD)], in_sem.at[2]
        ),
        pltpu.make_async_copy(prev, prv, in_sem.at[3]),
        pltpu.make_async_copy(acc, total, in_sem.at[4]),
    ]
    for copy in loads:
        copy.start()

    barrier = pltpu.get_barrier_semaphore()

    def greet(to):
        pl.semaphore_signal(
            barrier, inc=1, device_id={"domain": to[0], "band": to[1]}, device_id_type=MESH
        )

    for t in d_to:
        greet((t, b))
    greet((d, core_to))
    greet((d, x_to))

    @pl.when(has_up)
    def _():
        greet((d, z_up))

    @pl.when(has_down)
    def _():
        greet((d, z_down))

    peers = 2 + sides + jnp.where(has_up, 1, 0) + jnp.where(has_down, 1, 0)
    pl.semaphore_wait(barrier, peers)

    for i in range(min(WINDOW, count)):
        for s in range(sides):
            halo_copy(s, i).start()
    for copy in loads:
        copy.wait()

    shape = (planes, width)
    same_x = jnp.broadcast_to(sel[0], shape) != 0
    same_z = jnp.broadcast_to(sel[1], shape) != 0
    below = jnp.broadcast_to(sel[2], shape) != 0
    pieces = width // LANES

    def filter_chunk(i):
        o = i % orbs
        start = pl.multiple_of(i // orbs * width, LANES)
        wide = own[o, :, pl.ds(start, width + 2 * PAD)]
        half = pltpu.roll(wide, NX, 1)
        mid = wide[:, PAD : PAD + width]
        result = mid * ((pot[:, pl.ds(start, width)] - 36.0) * (1.0 / 14.0)) - load(prv, i)
        for step in range(1, REACH + 1):
            if step % 2 == 0:
                lo, hi, src = PAD - step * NX, PAD + step * NX, wide
            else:
                lo, hi, src = PAD - (step - 1) * NX, PAD + (step + 1) * NX, half
            result = result + scaled[step] * (src[:, lo : lo + width] + src[:, hi : hi + width])
        tall = jnp.concatenate(
            [mid[:, p * LANES : (p + 1) * LANES] for p in range(pieces)], axis=0
        )
        mixed = lax.dot_general(
            tall, xmat[...], (((1,), (0,)), ((), ())),
            precision=lax.Precision.HIGHEST, preferred_element_type=jnp.float32,
        )
        cols = []
        near = [load(halo.at[s], i) for s in range(sides)]
        for p in range(pieces):
            cut = slice(p * LANES, (p + 1) * LANES)
            col = result[:, cut] + mixed[p * planes : (p + 1) * planes]
            for q, src in enumerate([mid] + near):
                piece = src[:, cut]
                for r in range(planes):
                    turned = piece if r == 0 else pltpu.roll(piece, r, 0)
                    col = col + table[q, r] * turned
            cols.append(col)
        store(fil, i, jnp.concatenate(cols, axis=1))

    last_z = LAG_X + LAG_Z * (lines - 1)

    def inside(i):
        return (i >= 0) & (i < count)

    def step(t, carry):
        @pl.when(t < count)
        def _():
            for s in range(sides):
                halo_copy(s, t).wait_recv()

            @pl.when(t + WINDOW < count)
            def _():
                for s in range(sides):
                    halo_copy(s, t + WINDOW).start()

            filter_chunk(t)
            x_copy(t).start()
            out_copy(t).start()

        ix = t - LAG_X

        @pl.when(inside(ix))
        def _():
            x_copy(ix).wait_recv()
            store(from_x, ix, jnp.where(same_x, load(fil, ix), load(from_x, ix)))

        ir = t - LAG_X - LAG_Z * pz

        @pl.when(inside(ir))
        def _():
            @pl.when(has_down)
            def _():
                right_copy(ir).wait_recv()
                store(right, ir, jnp.where(same_z, load(from_x, ir), load(right, ir)))

            @pl.when(jnp.logical_not(has_down))
            def _():
                store(right, ir, load(from_x, ir))

            @pl.when(has_up)
            def _():
                right_copy(ir).start()

        il = t - LAG_X - LAG_Z * (lines - 1 - pz)

        @pl.when(inside(il))
        def _():
            @pl.when(has_up)
            def _():
                left_copy(il).wait_recv()
                store(left, il, jnp.where(same_z, load(from_x, il), load(left, il)))

            @pl.when(jnp.logical_not(has_up))
            def _():
                store(left, il, load(from_x, il))

            @pl.when(has_down)
            def _():
                left_copy(il).start()

        ib = t - last_z

        @pl.when(inside(ib))
        def _():
            store(block, ib, jnp.where(below, load(right, ib), load(left, ib)))
            core_copy(ib).start()

        ic = t - last_z - LAG_C

        @pl.when(inside(ic))
        def _():
            core_copy(ic).wait_recv()
            mine = load(block, ic)
            theirs = load(other, ic)
            o = ic % orbs
            part = pl.ds(pl.multiple_of(ic // orbs * width, LANES), width)
            for j in range(orbs):
                total[j, :, part] = total[j, :, part] + (
                    rows[core * orbs + o, j] * mine + rows[(1 - core) * orbs + o, j] * theirs
                )

        return carry

    lax.fori_loop(0, count + last_z + LAG_C, step, 0)
    for p in range(PARTS):
        total_copy(p).start()

    def drain(i, carry):
        for s in range(sides):
            halo_copy(s, i).wait_send()
        x_copy(i).wait_send()
        core_copy(i).wait_send()
        out_copy(i).wait()

        @pl.when(has_up)
        def _():
            right_copy(i).wait_send()

        @pl.when(has_down)
        def _():
            left_copy(i).wait_send()

        return carry

    lax.fori_loop(0, count, drain, 0)
    for p in range(PARTS):
        total_copy(p).wait()


def local(orbitals, previous, potential, rotation, accumulated, panel):
    domains = lax.axis_size("domain")
    bands = lax.axis_size("band")
    orbs, planes, cells = orbitals.shape
    pair = panel[0] % (bands // 2)
    rows = lax.dynamic_slice_in_dim(rotation, pair * 2 * orbs, 2 * orbs, 0)
    chip = lax.axis_index("band") // 2
    sel = jnp.stack(
        [pair % 2 == chip % 2, pair // 2 == chip // 2, pair // 2 <= chip // 2]
    ).astype(jnp.int32)
    table = jnp.asarray(z_tables(planes, domains))
    xmat = jnp.asarray(x_matrix())
    count = orbs * PARTS
    sides = 1 if domains == 2 else 2
    full = pltpu.VMEM(orbitals.shape, jnp.float32)
    dma = pltpu.SemaphoreType.DMA
    smem = pl.BlockSpec(memory_space=pltpu.SMEM)
    vmem = pl.BlockSpec(memory_space=pltpu.VMEM)
    hbm = pl.BlockSpec(memory_space=pl.ANY)
    shape = jax.ShapeDtypeStruct(orbitals.shape, jnp.float32)
    return pl.pallas_call(
        functools.partial(kernel, domains, bands),
        out_shape=(shape, shape),
        in_specs=[smem, smem, hbm, hbm, vmem, hbm, vmem, vmem],
        out_specs=(hbm, hbm),
        scratch_shapes=[
            pltpu.VMEM((orbs, planes, cells + 2 * PAD), jnp.float32),
            full,
            full,
            full,
            pltpu.VMEM((sides,) + orbitals.shape, jnp.float32),
            full, full, full, full, full,
            dma((5,)),
            dma((sides, count)), dma((sides, count)),
            dma((count,)), dma((count,)), dma((count,)), dma((count,)),
            dma((count,)), dma((count,)), dma((count,)), dma((count,)),
            dma((count,)), dma((PARTS,)),
        ],
        compiler_params=pltpu.CompilerParams(
            collective_id=0, has_side_effects=True, vmem_limit_bytes=48 * 1024 * 1024
        ),
        cost_estimate=pl.CostEstimate(
            flops=200 * orbs * planes * cells, bytes_accessed=40 * orbs * planes * cells,
            transcendentals=0,
        ),
    )(sel, rows, orbitals, previous, potential, accumulated, table, xmat)


def solution(mesh):
    in_specs = (
        P("band", "domain", None),
        P("band", "domain", None),
        P("domain", None),
        P(None, "band"),
        P("band", "domain", None),
        P(),
    )
    out_specs = (P("band", "domain", None), P("band", "domain", None))
    return jax.shard_map(local, mesh=mesh, in_specs=in_specs, out_specs=out_specs, check_vma=False)
```

time: 251 us -> 88 us (0.35)
  waiting for transfers between devices: 119 us -> 0 us
  Pallas kernels: 0 us -> 80.9 us
  local copies, waits for them, and re-layouts: 79.3 us -> 5.39 us
  other arithmetic: 26.6 us -> 0.08 us
  between operations: 14.9 us -> 1.39 us
  matrix products: 7.3 us -> 0 us
    psum x1 -> x0, waiting for transfers between devices: 112 us -> none  [from_root(): return lax.psum(block, axis)]
    pallas_call x0 -> x1, Pallas kernels: none -> 80.9 us  [local(): pl.pallas_call(functools.partial(kernel, domains, bands), out_shape=(shap...]
    slice x37 -> x0, local copies, waits for them, and re-layouts: 61.2 us -> none  [the longest x12 20.7 us: shift_x(): jnp.roll(values, amount, 2)]
    select_n x2 -> x0, other arithmetic: 26.6 us -> none  [from_root(): jnp.where(lax.axis_index(axis) == owner, block, jnp.zeros_like(block))]
    dot_general x2 -> x0, matrix products: 7.3 us -> none  [add_panel(): lax.dot_general(rows, flat, (((0,), (0,)), ((), ())), precision=lax.Preci...]
    ppermute x2 -> x0, waiting for transfers between devices: 6.54 us -> none  [the longest x1 6.53 us: padded_2(): lax.ppermute(tail, axis, [(i, (i + 1) % count) for i in range(count)])]
    dot_general x2 -> x0, local copies, waits for them, and re-layouts: 5.1 us -> none  [add_panel(): lax.dot_general(rows, flat, (((0,), (0,)), ((), ())), precision=lax.Preci...]
    unnamed x16 -> x11, local copies, waits for them, and re-layouts: 8.03 us -> 5.31 us
  transfers between devices with their start and end apart: 3 -> 0, of which waited for: 2 -> 0; matrix products, arithmetic and copies ran while one was open for 25% -> 0% of each run, Pallas kernels for 0% -> 0%
where the time goes in v1:
time: 88 us; the launch traced here: 87.8 us
  Pallas kernels  80.9 us (92%)
  local copies, waits for them, and re-layouts  5.39 us (6%)
  between operations  1.39 us (2%)
    pallas_call x1, Pallas kernels, local(): pl.pallas_call(functools.partial(kernel, domains, bands), out_shape=(shap...  80.9 us
    unnamed x11, local copies, waits for them, and re-layouts  5.31 us

profile of v1, /device:TPU:1, one launch (start us, length us, event | category | flops | bytes accessed | tf_op | source)
XLA Modules:
  0.0 87.8 jit_solution(1515603549135792615)
XLA Ops:
  0.6 0.0 copy-start
  1.4 0.1 add_convert_fusion.sel
  1.5 0.0 copy-done
  1.5 0.1 constant_dynamic-slice_fusion
  1.5 0.1 copy.11.rows
  1.6 0.0 copy-start.1
  1.6 0.9 %copy-done.1 = f32[8,4096]{1,0:T(8,128)S(1)} copy-done((f32[8,4096]{1,0:T(8,128)S(1)}, f32[8,4096]{1,0:T(8,128)}, u32[]{:S(2)}) %copy-start.1) | copy-done | bytes 131096
  2.5 0.0 copy-start.2
  2.5 0.8 copy-done.2
  3.4 0.0 copy-start.3
  3.4 0.8 copy-done.3
  4.2 80.9 %shard_map.95 = (f32[16,8,4096]{2,1,0:T(8,128)S(1)}, f32[16,8,4096]{2,1,0:T(8,128)S(1)}) custom-call(s32[3]{0:T(128)S(1)} %add_convert_fusion.sel, f32[32,16]{1,0:T(8,128)S(1)} %copy.11.rows, f32[16,8,4096]{2,1,0:T(8,128)} %orb.1, f32[16,8,4096]{2,1,0:T(8,128)} %prev.1, f32[8,4096]{1,0:T(8,128)S(1)} %copy-done.1, f32[16,8,4096]{2,1,0:T(8,128)} %acc.1, ...), custom_call_target="tpu_custom_call" | custom-call | flops 104857600 | bytes 20971520 | tf_op jit(solution)/shard_map/pallas_call | solution.py:342
  85.1 1.3 %copy.15 = f32[16,8,4096]{2,1,0:T(8,128)} copy(f32[16,8,4096]{2,1,0:T(8,128)S(1)} %get-tuple-element.4) | data formatting | bytes 4194304
  86.4 1.3 %copy.16 = f32[16,8,4096]{2,1,0:T(8,128)} copy(f32[16,8,4096]{2,1,0:T(8,128)S(1)} %get-tuple-element.5) | data formatting | bytes 4194304
Async XLA Ops:
  0.6 0.8 copy-start
  1.6 0.9 %copy-start.1 = (f32[8,4096]{1,0:T(8,128)S(1)}, f32[8,4096]{1,0:T(8,128)}, u32[]{:S(2)}) copy-start(f32[8,4096]{1,0:T(8,128)} %pot.1) | copy-start | bytes 393220
  2.5 0.8 copy-start.2
  3.4 0.8 copy-start.3

commit v2 on v1

--- a/solution.py
+++ b/solution.py
@@ -14,8 +14,8 @@
 PAD = REACH * NX
 PARTS = 2
 WINDOW = 6
-LAG_X = 2
-LAG_Z = 2
+LAG_X = 3
+LAG_Z = 3
 LAG_C = 2
 MESH = pl.DeviceIdType.MESH
 

time: 88 us -> 80.2 us (0.911)
  Pallas kernels: 80.9 us -> 73.1 us
    pallas_call x1, Pallas kernels: 80.9 us -> 73.1 us  [local(): pl.pallas_call(functools.partial(kernel, domains, bands), out_shape=(shap...]
where the time goes in v2:
time: 80.2 us; the launch traced here: 79.9 us
  Pallas kernels  73.1 us (91%)
  local copies, waits for them, and re-layouts  5.39 us (7%)
  between operations  1.39 us (2%)
    pallas_call x1, Pallas kernels, local(): pl.pallas_call(functools.partial(kernel, domains, bands), out_shape=(shap...  73.1 us
    unnamed x11, local copies, waits for them, and re-layouts  5.31 us

profile of v2, /device:TPU:1, one launch (start us, length us, event | category | flops | bytes accessed | tf_op | source)
XLA Modules:
  0.0 79.9 jit_solution(3767553282890134056)
XLA Ops:
  0.6 0.0 copy-start
  1.4 0.1 add_convert_fusion.sel
  1.5 0.0 copy-done
  1.5 0.1 constant_dynamic-slice_fusion
  1.5 0.1 copy.11.rows
  1.6 0.0 copy-start.1
  1.6 0.9 %copy-done.1 = f32[8,4096]{1,0:T(8,128)S(1)} copy-done((f32[8,4096]{1,0:T(8,128)S(1)}, f32[8,4096]{1,0:T(8,128)}, u32[]{:S(2)}) %copy-start.1) | copy-done | bytes 131096
  2.5 0.0 copy-start.2
  2.5 0.8 %copy-done.2 = f32[128,128]{1,0:T(8,128)S(1)} copy-done((f32[128,128]{1,0:T(8,128)S(1)}, f32[128,128]{1,0:T(8,128)}, u32[]{:S(2)}) %copy-start.2) | copy-done | bytes 65560
  3.4 0.0 copy-start.3
  3.4 0.8 %copy-done.3 = f32[2,8,8,128]{3,2,1,0:T(8,128)S(1)} copy-done((f32[2,8,8,128]{3,2,1,0:T(8,128)S(1)}, f32[2,8,8,128]{3,2,1,0:T(8,128)}, u32[]{:S(2)}) %copy-start.3) | copy-done | bytes 65560
  4.2 73.1 %shard_map.95 = (f32[16,8,4096]{2,1,0:T(8,128)S(1)}, f32[16,8,4096]{2,1,0:T(8,128)S(1)}) custom-call(s32[3]{0:T(128)S(1)} %add_convert_fusion.sel, f32[32,16]{1,0:T(8,128)S(1)} %copy.11.rows, f32[16,8,4096]{2,1,0:T(8,128)} %orb.1, f32[16,8,4096]{2,1,0:T(8,128)} %prev.1, f32[8,4096]{1,0:T(8,128)S(1)} %copy-done.1, f32[16,8,4096]{2,1,0:T(8,128)} %acc.1, ...), custom_call_target="tpu_custom_call" | custom-call | flops 104857600 | bytes 20971520 | tf_op jit(solution)/shard_map/pallas_call | solution.py:342
  77.3 1.3 %copy.15 = f32[16,8,4096]{2,1,0:T(8,128)} copy(f32[16,8,4096]{2,1,0:T(8,128)S(1)} %get-tuple-element.4) | data formatting | bytes 4194304
  78.6 1.3 %copy.16 = f32[16,8,4096]{2,1,0:T(8,128)} copy(f32[16,8,4096]{2,1,0:T(8,128)S(1)} %get-tuple-element.5) | data formatting | bytes 4194304
Async XLA Ops:
  0.6 0.8 %copy-start = (f32[256,16]{0,1:T(8,128)S(1)}, f32[256,16]{0,1:T(8,128)}, u32[]{:S(2)}) copy-start(f32[256,16]{0,1:T(8,128)} %param.11) | copy-start | bytes 49156
  1.6 0.9 %copy-start.1 = (f32[8,4096]{1,0:T(8,128)S(1)}, f32[8,4096]{1,0:T(8,128)}, u32[]{:S(2)}) copy-start(f32[8,4096]{1,0:T(8,128)} %pot.1) | copy-start | bytes 393220
  2.5 0.8 %copy-start.2 = (f32[128,128]{1,0:T(8,128)S(1)}, f32[128,128]{1,0:T(8,128)}, u32[]{:S(2)}) copy-start(f32[128,128]{1,0:T(8,128)} %constant.73.clone.xmat) | copy-start | bytes 196612
  3.4 0.8 %copy-start.3 = (f32[2,8,8,128]{3,2,1,0:T(8,128)S(1)}, f32[2,8,8,128]{3,2,1,0:T(8,128)}, u32[]{:S(2)}) copy-start(f32[2,8,8,128]{3,2,1,0:T(8,128)} %constant.72.clone.table) | copy-start | bytes 196612

commit v3 on v2

--- a/solution.py
+++ b/solution.py
@@ -167,7 +167,7 @@
     for i in range(min(WINDOW, count)):
         for s in range(sides):
             halo_copy(s, i).start()
-    for copy in loads:
+    for copy in loads[:4]:
         copy.wait()
 
     shape = (planes, width)
@@ -215,6 +215,58 @@
         return (i >= 0) & (i < count)
 
     def step(t, carry):
+        @pl.when(t == 1)
+        def _():
+            loads[4].wait()
+
+        ix = t - LAG_X
+
+        @pl.when(inside(ix))
+        def _():
+            x_copy(ix).wait_recv()
+            store(from_x, ix, jnp.where(same_x, load(fil, ix), load(from_x, ix)))
+
+        ir = t - LAG_X - LAG_Z * pz
+
+        @pl.when(inside(ir))
+        def _():
+            @pl.when(has_down)
+            def _():
+                right_copy(ir).wait_recv()
+                store(right, ir, jnp.where(same_z, load(from_x, ir), load(right, ir)))
+
+            @pl.when(jnp.logical_not(has_down))
+            def _():
+                store(right, ir, load(from_x, ir))
+
+            @pl.when(has_up)
+            def _():
+                right_copy(ir).start()
+
+        il = t - LAG_X - LAG_Z * (lines - 1 - pz)
+
+        @pl.when(inside(il))
+        def _():
+            @pl.when(has_up)
+            def _():
+                left_copy(il).wait_recv()
+                store(left, il, jnp.where(same_z, load(from_x, il), load(left, il)))
+
+            @pl.when(jnp.logical_not(has_up))
+            def _():
+                store(left, il, load(from_x, il))
+
+            @pl.when(has_down)
+            def _():
+                left_copy(il).start()
+
+        ib = t - last_z
+
+        @pl.when(inside(ib))
+        def _():
+            store(block, ib, jnp.where(below, load(right, ib), load(left, ib)))
+            core_copy(ib).start()
+
         @pl.when(t < count)
         def _():
             for s in range(sides):
@@ -228,54 +280,6 @@
             filter_chunk(t)
             x_copy(t).start()
             out_copy(t).start()
-
-        ix = t - LAG_X
-
-        @pl.when(inside(ix))
-        def _():
-            x_copy(ix).wait_recv()
-            store(from_x, ix, jnp.where(same_x, load(fil, ix), load(from_x, ix)))
-
-        ir = t - LAG_X - LAG_Z * pz
-
-        @pl.when(inside(ir))
-        def _():
-            @pl.when(has_down)
-            def _():
-                right_copy(ir).wait_recv()
-                store(right, ir, jnp.where(same_z, load(from_x, ir), load(right, ir)))
-
-            @pl.when(jnp.logical_not(has_down))
-            def _():
-                store(right, ir, load(from_x, ir))
-
-            @pl.when(has_up)
-            def _():
-                right_copy(ir).start()
-
-        il = t - LAG_X - LAG_Z * (lines - 1 - pz)
-
-        @pl.when(inside(il))
-        def _():
-            @pl.when(has_up)
-            def _():
-                left_copy(il).wait_recv()
-                store(left, il, jnp.where(same_z, load(from_x, il), load(left, il)))
-
-            @pl.when(jnp.logical_not(has_up))
-            def _():
-                store(left, il, load(from_x, il))
-
-            @pl.when(has_down)
-            def _():
-                left_copy(il).start()
-
-        ib = t - last_z
-
-        @pl.when(inside(ib))
-        def _():
-            store(block, ib, jnp.where(below, load(right, ib), load(left, ib)))
-            core_copy(ib).start()
 
         ic = t - last_z - LAG_C
 

time: 80.2 us -> 79.6 us (level)
  no operation moved by 1% of the time
where the time goes in v3:
time: 79.6 us; the launch traced here: 79.3 us
  Pallas kernels  72.5 us (91%)
  local copies, waits for them, and re-layouts  5.39 us (7%)
  between operations  1.39 us (2%)
    pallas_call x1, Pallas kernels, local(): pl.pallas_call(functools.partial(kernel, domains, bands), out_shape=(shap...  72.5 us
    unnamed x11, local copies, waits for them, and re-layouts  5.31 us

profile of v3, /device:TPU:1, one launch (start us, length us, event | category | flops | bytes accessed | tf_op | source)
XLA Modules:
  0.0 79.3 jit_solution(4327161804396932511)
XLA Ops:
  0.6 0.0 copy-start
  1.4 0.1 add_convert_fusion.sel
  1.5 0.0 copy-done
  1.5 0.1 constant_dynamic-slice_fusion
  1.5 0.1 copy.11.rows
  1.6 0.0 copy-start.1
  1.6 0.9 %copy-done.1 = f32[8,4096]{1,0:T(8,128)S(1)} copy-done((f32[8,4096]{1,0:T(8,128)S(1)}, f32[8,4096]{1,0:T(8,128)}, u32[]{:S(2)}) %copy-start.1) | copy-done | bytes 131096
  2.5 0.0 copy-start.2
  2.5 0.8 %copy-done.2 = f32[128,128]{1,0:T(8,128)S(1)} copy-done((f32[128,128]{1,0:T(8,128)S(1)}, f32[128,128]{1,0:T(8,128)}, u32[]{:S(2)}) %copy-start.2) | copy-done | bytes 65560
  3.4 0.0 copy-start.3
  3.4 0.8 %copy-done.3 = f32[2,8,8,128]{3,2,1,0:T(8,128)S(1)} copy-done((f32[2,8,8,128]{3,2,1,0:T(8,128)S(1)}, f32[2,8,8,128]{3,2,1,0:T(8,128)}, u32[]{:S(2)}) %copy-start.3) | copy-done | bytes 65560
  4.2 72.5 %shard_map.95 = (f32[16,8,4096]{2,1,0:T(8,128)S(1)}, f32[16,8,4096]{2,1,0:T(8,128)S(1)}) custom-call(s32[3]{0:T(128)S(1)} %add_convert_fusion.sel, f32[32,16]{1,0:T(8,128)S(1)} %copy.11.rows, f32[16,8,4096]{2,1,0:T(8,128)} %orb.1, f32[16,8,4096]{2,1,0:T(8,128)} %prev.1, f32[8,4096]{1,0:T(8,128)S(1)} %copy-done.1, f32[16,8,4096]{2,1,0:T(8,128)} %acc.1, ...), custom_call_target="tpu_custom_call" | custom-call | flops 104857600 | bytes 20971520 | tf_op jit(solution)/shard_map/pallas_call | solution.py:346
  76.7 1.3 %copy.15 = f32[16,8,4096]{2,1,0:T(8,128)} copy(f32[16,8,4096]{2,1,0:T(8,128)S(1)} %get-tuple-element.4) | data formatting | bytes 4194304
  78.0 1.3 %copy.16 = f32[16,8,4096]{2,1,0:T(8,128)} copy(f32[16,8,4096]{2,1,0:T(8,128)S(1)} %get-tuple-element.5) | data formatting | bytes 4194304
Async XLA Ops:
  0.6 0.8 %copy-start = (f32[256,16]{0,1:T(8,128)S(1)}, f32[256,16]{0,1:T(8,128)}, u32[]{:S(2)}) copy-start(f32[256,16]{0,1:T(8,128)} %param.11) | copy-start | bytes 49156
  1.6 0.9 %copy-start.1 = (f32[8,4096]{1,0:T(8,128)S(1)}, f32[8,4096]{1,0:T(8,128)}, u32[]{:S(2)}) copy-start(f32[8,4096]{1,0:T(8,128)} %pot.1) | copy-start | bytes 393220
  2.5 0.8 %copy-start.2 = (f32[128,128]{1,0:T(8,128)S(1)}, f32[128,128]{1,0:T(8,128)}, u32[]{:S(2)}) copy-start(f32[128,128]{1,0:T(8,128)} %constant.73.clone.xmat) | copy-start | bytes 196612
  3.4 0.8 %copy-start.3 = (f32[2,8,8,128]{3,2,1,0:T(8,128)S(1)}, f32[2,8,8,128]{3,2,1,0:T(8,128)}, u32[]{:S(2)}) copy-start(f32[2,8,8,128]{3,2,1,0:T(8,128)} %constant.72.clone.table) | copy-start | bytes 196612
